TPU v7x, 512 devices: a whole 4x8x8 slice. The times are simulated.
512 devices in a mesh: rep: 32 (over z, x_lo, core), fsdp: 16 (over x_hi, y).
Axes of the slice: x: 4 (x_hi: 2, x_lo: 2; x = x_hi * 2 + x_lo), y: 8, z: 8, core: 2. Of those that a mesh axis runs over, the one named last changes fastest.
Arguments:
- acts: bfloat16 [65536, 64], P(('rep', 'fsdp')), may hold values from -16 to 16
- cotangent: bfloat16 [65536, 14336], P(('rep', 'fsdp')), may hold values from -0.125 to 0.125
- weight: float32 [64, 14336], P('fsdp'), may hold values from -0.0625 to 0.0625
- momentum: float32 [32, 64, 14336], P('rep', 'fsdp'), may hold values from -6 to 6
- bands: int32 [64, 4], P('fsdp'), may hold values from 0 to 63, all different within a row
Outputs:
- new_weight: float32 [64, 14336], P('fsdp')
- new_momentum: float32 [32, 64, 14336], P('rep', 'fsdp')
Inputs may be any that keep to these rules, and one draw needn't show every extreme that they name: Each row of the window names 4 different bands, and every band is named by some row.
All inputs are finite; a program needn't handle non-finite values.
Results may differ from a plain program's by a relative error of at most 0.0003.
Values sent between devices are 32-bit elements; how exact they have to be, the bound alone decides.
A program may use at most 64 MiB of HBM per device.

v0:
```python
import jax
import jax.numpy as jnp
from jax import lax
from jax.sharding import PartitionSpec as P

BAND = 64


step_size = 2.0
decay = 0.999


def dct_table(width):
    index = jnp.arange(width, dtype=jnp.int32)
    freq = index.astype(jnp.float32)[:, None]
    place = index.astype(jnp.float32)[None, :]
    table = jnp.cos(jnp.pi * (2.0 * place + 1.0) * freq / (2.0 * width))
    scale = jnp.where(index == 0, jnp.sqrt(1.0 / width), jnp.sqrt(2.0 / width)).astype(jnp.float32)
    return table * scale[:, None]


def pick_rows(bands, width):
    onehot = (bands[:, :, None] == jnp.arange(width, dtype=jnp.int32)[None, None, :]).astype(
        jnp.float32
    )
    return jnp.einsum("rkm,mj->rkj", onehot, dct_table(width), precision=lax.Precision.HIGHEST)


def on_device(acts, cotangent, weight, momentum, bands):
    rows = weight.shape[0]
    width = cotangent.shape[1]
    contract = (((0,), (0,)), ((), ()))
    term = lax.dot_general(acts, cotangent, contract, preferred_element_type=jnp.float32)
    grad = lax.psum_scatter(term, "fsdp", scatter_dimension=0, tiled=True)
    moved = decay * momentum[0] + grad
    picks = pick_rows(bands, BAND)
    blocks = moved.reshape(rows, width // BAND, BAND)
    coefs = jnp.einsum("rcj,rkj->rkc", blocks, picks, precision=lax.Precision.HIGHEST)
    own = jnp.einsum("rkc,rkj->rcj", coefs, picks, precision=lax.Precision.HIGHEST)
    new_momentum = (moved - own.reshape(rows, width))[None]
    total = lax.psum(coefs, "rep")
    mean = total / lax.axis_size("rep")
    update = jnp.einsum("rkc,rkj->rcj", mean, picks, precision=lax.Precision.HIGHEST).reshape(
        rows, width
    )
    new_weight = weight - step_size * update
    return (new_weight, new_momentum)


def solution(mesh):
    placed = (
        P(("rep", "fsdp"), None),
        P(("rep", "fsdp"), None),
        P("fsdp", None),
        P("rep", "fsdp", None),
        P("fsdp", None),
    )
    return jax.shard_map(
        on_device,
        mesh=mesh,
        in_specs=placed,
        out_specs=(P("fsdp", None), P("rep", "fsdp", None)),
        check_vma=False,
    )
```

profile of v0, /device:TPU:1, one launch (start us, length us, event | category | flops | bytes accessed | tf_op | source)
XLA Modules:
  0.0 308.6 jit_solution(10914312742562734719)
XLA Ops:
  7.2 0.0 copy-start
  7.2 0.0 all-reduce.3.cloned.1.call-start
  7.2 0.7 copy-done
  7.9 4.5 %fusion.15 = f32[64,14336]{1,0:T(8,128)} fusion(bf16[128,64]{0,1:T(8,128)(2,1)S(1)} %copy-done, bf16[128,14336]{1,0:T(8,128)(2,1)} %param.6), kind=kOutput, calls=%fused_computation.22 | convolution fusion | flops 234881024 | bytes 7356416 | tf_op jit(solution)/shard_map/dot_general | solution.py:33
  12.4 0.0 copy-start.3
  12.4 0.0 copy-start.1
  12.4 0.0 all-reduce.3.cloned.1.call-update
  12.4 0.0 copy-start.2
  12.4 1.4 dynamic-slice
  14.5 0.0 copy-done.3
  14.5 0.3 fusion
  14.8 170.5 %all-reduce.3.cloned.1.call-done = f32[64,14336]{1,0:T(8,128)} async-done(((f32[64,14336]{1,0:T(8,128)}), f32[64,14336]{1,0:T(8,128)}) %all-reduce.3.cloned.1.call-update) | async-done | bytes 3670032
  185.4 0.0 copy-done.1
  185.4 1.1 dynamic-slice_add_fusion
  186.5 0.3 reshape.35
  186.7 0.8 fusion.16
  187.6 0.9 fusion.17
  188.5 110.7 %psum.7 = f32[4,4,224]{2,1,0:T(4,128)S(1)} all-reduce(f32[4,4,224]{2,1,0:T(4,128)S(1)} %fusion.16), channel_id=1, replica_groups=mesh['rep'=32,'fsdp'=16] {'rep'}, use_global_device_ids=true, to_apply=%region_1.2 | all-reduce | flops 3584 | bytes 28672 | tf_op jit(solution)/shard_map/psum | solution.py:41
  299.2 0.2 reshape.36
  299.4 0.7 subtract_bitcast_fusion
  300.1 0.4 convolution_multiply_fusion
  300.6 0.2 copy.13
  300.7 0.2 mul.75
  301.0 0.0 copy-done.2
  301.0 0.7 sub.6
  (2 shorter events, 0.0 us)
Async XLA Ops:
  7.2 0.7 copy-start
  7.2 178.2 %all-reduce.3.cloned.1.call-start = ((), (), s32[]{:S(2)}) async-start(), calls=%async_computation | async-start | bytes 7340032
  12.4 2.1 copy-start.3
  12.4 173.0 %copy-start.1 = (f32[1,4,14336]{2,1,0:T(4,128)S(1)}, f32[1,4,14336]{2,1,0:T(4,128)}, u32[]{:S(2)}) copy-start(f32[1,4,14336]{2,1,0:T(4,128)} %param.8) | copy-start | bytes 688132
  12.4 288.5 %copy-start.2 = (f32[4,14336]{1,0:T(4,128)S(1)}, f32[4,14336]{1,0:T(4,128)}, u32[]{:S(2)}) copy-start(f32[4,14336]{1,0:T(4,128)} %param.7) | copy-start | bytes 688132
Sparse Core Ops, SparseCore 0:
  12.5 172.7 all-reduce.2
where the time goes:
time: 311 us; the launch traced here: 309 us
  waiting for transfers between devices  171 us (55%)
  blocking collectives  111 us (36%)
  between operations  14.8 us (5%)
  matrix products  7.02 us (2%)
    unnamed x2, waiting for transfers between devices  171 us
    psum x1, blocking collectives, on_device(): total = lax.psum(coefs, 'rep')  111 us
  transfers between devices with their start and end apart: 1, of which 1 were waited for; matrix products, arithmetic and copies ran while one was open for 1% of the time, Pallas kernels for 0%

commit v1 on v0

v1 whole, which is shorter than its diff:
```python
import jax
import jax.numpy as jnp
import numpy as np
from jax import lax
from jax.experimental import pallas as pl
from jax.experimental.pallas import tpu as pltpu
from jax.sharding import PartitionSpec as P

MESH = pl.DeviceIdType.MESH
F32, BF16 = jnp.float32, jnp.bfloat16

TOK, COLS, ROWS, BAND, KEEP = 128, 14336, 64, 64, 4
NZ, NY = 8, 8
OWN = 4
GROUP = 2048
GROUPS = COLS // GROUP
HALF = GROUP // 2
CHUNK = 512
TILES = GROUP // 128

STEP_SIZE = 2.0
DECAY = 0.999

UNITS = (
    [(3, 0), (3, 1), (4, 0), (4, 1), (-3, 0), (-3, 1)]
    + [(d, 1) for d in (-2, -1, 0, 1, 2)]
    + [(d, 0) for d in (-2, -1, 0, 1, 2)]
)
FAR_P, OPP, FAR_M = 0, 2, 4
CROSS = 6
HERE = 11


def table():
    band, place = np.arange(BAND)[None, :], np.arange(2 * BAND)[:, None] % BAND
    scale = np.where(band == 0, np.sqrt(1.0 / BAND), np.sqrt(2.0 / BAND))
    full = (scale * np.cos(np.pi * (2 * place + 1) * band / (2 * BAND))).astype(np.float32)
    high = full.astype(jnp.bfloat16)
    low = (full - high.astype(np.float32)).astype(jnp.bfloat16)
    return np.stack([high, low])


def cols_of(g, half=None):
    if half is None:
        return pl.ds(g * GROUP, GROUP)
    return pl.ds(g * GROUP + half * HALF, HALF)


def split(x):
    high = x.astype(BF16)
    return high, (x - high.astype(F32)).astype(BF16)


def by_row(x, row):
    return jnp.concatenate([jnp.where(row == i, x, 0.0) for i in range(OWN)], axis=1)


def kernel(
    bands, acts_hbm, cot_hbm, weight_hbm, momentum_hbm, table_hbm,
    new_weight, new_momentum,
    acts, cot, weight, momentum, tab, out_w, out_m,
    term, got4, got3p, got3m, gotx, got2p, got2m, got1p, got1m,
    wa_hi, wa_lo, wb_hi, wb_lo, quad, ring,
    load_sem, cot_sem, store_sem, send, recv, quad_send, quad_recv, ring_send, ring_recv,
):
    rep, fsdp = lax.axis_index("rep"), lax.axis_index("fsdp")
    z, me4 = rep // 4, lax.rem(rep, 4)
    xlo, core = me4 // 2, lax.rem(me4, 2)
    xhi, y = fsdp // NY, lax.rem(fsdp, NY)

    up = (rep, xhi * NY + lax.rem(y + 1, NY))
    down = (rep, xhi * NY + lax.rem(y + NY - 1, NY))
    across = (rep, (1 - xhi) * NY + y)
    quads = [
        (z * 4 + 2 * xlo + (1 - core), fsdp),
        (z * 4 + 2 * (1 - xlo) + core, fsdp),
        (z * 4 + 2 * (1 - xlo) + (1 - core), fsdp),
    ]
    rings = [(lax.rem(z + t, NZ) * 4 + me4, fsdp) for t in range(1, NZ)]

    loads = []
    for i, (src, dst) in enumerate(
        [(acts_hbm, acts), (table_hbm, tab), (momentum_hbm, momentum), (weight_hbm, weight)]
    ):
        loads.append(pltpu.make_async_copy(src, dst, load_sem.at[i]))
    cots = [
        pltpu.make_async_copy(cot_hbm.at[:, cols_of(g)], cot.at[:, cols_of(g)], cot_sem.at[g])
        for g in range(GROUPS)
    ]
    loads[0].start()
    cots[0].start()
    loads[1].start()
    for c in cots[1:]:
        c.start()
    loads[2].start()
    loads[3].start()

    barrier = pltpu.get_barrier_semaphore()
    friends = [up, down, across, *quads, *rings]
    for d in friends:
        pl.semaphore_signal(barrier, inc=1, device_id=d, device_id_type=MESH)

    sent = []
    counter = [0]

    def message(src, dst, device):
        n = counter[0]
        counter[0] += 1
        c = pltpu.make_async_remote_copy(
            src_ref=src, dst_ref=dst, send_sem=send.at[n], recv_sem=recv.at[n],
            device_id=device, device_id_type=MESH,
        )
        c.start()
        sent.append(c)
        return c

    loads[0].wait()
    place = lax.broadcasted_iota(jnp.int32, (ROWS, ROWS), 0)
    unit, sub = place // OWN, lax.rem(place, OWN)
    wanted = jnp.zeros((ROWS, ROWS), jnp.int32)
    for u, (d, r) in enumerate(UNITS):
        side = xhi if r == 0 else 1 - xhi
        owner = side * NY + lax.rem(y + d + NY, NY)
        wanted = jnp.where(unit == u, owner * OWN + sub, wanted)
    order = (wanted == lax.broadcasted_iota(jnp.int32, (ROWS, ROWS), 1)).astype(BF16)
    acts_t = lax.dot_general(
        order, acts[...], (((1,), (1,)), ((), ())), preferred_element_type=F32
    ).astype(BF16)

    m = {}

    def products(g):
        cots[g].wait()
        for s in range(GROUP // CHUNK):
            at = pl.ds(g * GROUP + s * CHUNK, CHUNK)
            out = jnp.dot(acts_t, cot[:, at], preferred_element_type=F32)
            for u in range(16):
                term[u, :, at] = out[u * OWN : (u + 1) * OWN]

    def first_sends(g):
        e, o = cols_of(g, 0), cols_of(g, 1)
        m["4p", g] = message(term.at[pl.ds(OPP, 2), :, e], got4.at[:, :, e], up)
        m["4m", g] = message(term.at[pl.ds(OPP, 2), :, o], got4.at[:, :, o], down)
        m["3p", g, 1] = message(term.at[pl.ds(FAR_P, 2), :, o], got3p.at[:, :, o], up)
        m["3m", g, 0] = message(term.at[pl.ds(FAR_M, 2), :, e], got3m.at[:, :, e], down)

    def x_one(g):
        c = cols_of(g)
        m["x1p", g] = message(term.at[CROSS + 3, :, c], gotx.at[3, :, c], across)
        m["x1m", g] = message(term.at[CROSS + 1, :, c], gotx.at[1, :, c], across)

    def x_zero(g):
        c = cols_of(g)
        m["x0", g] = message(term.at[CROSS + 2, :, c], gotx.at[2, :, c], across)

    def step_b(g):
        e, o = cols_of(g, 0), cols_of(g, 1)
        m["4p", g].wait_recv()
        term[FAR_P : FAR_P + 2, :, e] += got4[:, :, e]
        m["3p", g, 0] = message(term.at[pl.ds(FAR_P, 2), :, e], got3p.at[:, :, e], up)
        m["4m", g].wait_recv()
        term[FAR_M : FAR_M + 2, :, o] += got4[:, :, o]
        m["3m", g, 1] = message(term.at[pl.ds(FAR_M, 2), :, o], got3m.at[:, :, o], down)

    def step_c(g, free):
        hp, hm = (1, 0) if free else (0, 1)
        c = cols_of(g, hp)
        m["3p", g, hp].wait_recv()
        term[CROSS + 4, :, c] += got3p[1, :, c]
        m["x2p", g, hp] = message(term.at[CROSS + 4, :, c], gotx.at[4, :, c], across)
        term[HERE + 4, :, c] += got3p[0, :, c]
        c = cols_of(g, hm)
        m["3m", g, hm].wait_recv()
        term[CROSS, :, c] += got3m[1, :, c]
        m["x2m", g, hm] = message(term.at[CROSS, :, c], gotx.at[0, :, c], across)
        term[HERE, :, c] += got3m[0, :, c]

    def step_d(g):
        c = cols_of(g)
        m["x2p", g, 0].wait_recv()
        m["x2p", g, 1].wait_recv()
        term[HERE + 4, :, c] += gotx[4, :, c]
        m["2p", g] = message(term.at[HERE + 4, :, c], got2p.at[:, c], up)
        m["x2m", g, 0].wait_recv()
        m["x2m", g, 1].wait_recv()
        term[HERE, :, c] += gotx[0, :, c]
        m["2m", g] = message(term.at[HERE, :, c], got2m.at[:, c], down)

    def step_e(g):
        c = cols_of(g)
        m["x1p", g].wait_recv()
        m["2p", g].wait_recv()
        term[HERE + 3, :, c] += got2p[:, c] + gotx[3, :, c]
        m["1p", g] = message(term.at[HERE + 3, :, c], got1p.at[:, c], up)
        m["x1m", g].wait_recv()
        m["2m", g].wait_recv()
        term[HERE + 1, :, c] += got2m[:, c] + gotx[1, :, c]
        m["1m", g] = message(term.at[HERE + 1, :, c], got1m.at[:, c], down)

    row = lax.rem(lax.broadcasted_iota(jnp.int32, (OWN * TILES, 128), 0), OWN)
    tile = lax.broadcasted_iota(jnp.int32, (OWN * TILES, 128), 0) // OWN
    lane8 = lax.broadcasted_iota(jnp.int32, (OWN * TILES, 128), 1) // (2 * KEEP)
    mine = tile == lane8

    def picks():
        loads[1].wait()
        lane = lax.broadcasted_iota(jnp.int32, (BAND, 128), 1)
        band = lax.broadcasted_iota(jnp.int32, (BAND, 128), 0)
        c = lax.broadcasted_iota(jnp.int32, (128, 128), 0)
        l = lax.broadcasted_iota(jnp.int32, (128, 128), 1)
        same = c // BAND == lax.rem(l // KEEP, 2)
        for i in range(OWN):
            want = jnp.zeros((BAND, 128), jnp.int32)
            for k in range(KEEP):
                want = jnp.where(lax.rem(lane, KEEP) == k, bands[i, k], want)
            onehot = (want == band).astype(BF16)
            for t, wa, wb in ((0, wa_hi, wb_hi), (1, wa_lo, wb_lo)):
                w = jnp.dot(tab[t], onehot, preferred_element_type=F32)
                w = jnp.where(same, w, 0.0).astype(BF16)
                wa[i * 128 : (i + 1) * 128, :] = w
                wb[:, i * 128 : (i + 1) * 128] = w

    def spread(coefs):
        hi, lo = split(by_row(coefs, row))
        nt = (((1,), (1,)), ((), ()))
        out = lax.dot_general(hi, wb_hi[...], nt, preferred_element_type=F32)
        out += lax.dot_general(hi, wb_lo[...], nt, preferred_element_type=F32)
        out += lax.dot_general(lo, wb_hi[...], nt, preferred_element_type=F32)
        return jnp.concatenate([out[j * OWN : (j + 1) * OWN] for j in range(TILES)], axis=1)

    stores = []

    def step_f(g):
        c = cols_of(g)
        m["x0", g].wait_recv()
        m["1p", g].wait_recv()
        m["1m", g].wait_recv()
        grad = (term[HERE + 2, :, c] + gotx[2, :, c]) + (got1p[:, c] + got1m[:, c])
        moved = DECAY * momentum[0, :, c] + grad
        x = jnp.concatenate([moved[:, j * 128 : (j + 1) * 128] for j in range(TILES)], axis=0)
        hi, lo = split(by_row(x, row))
        coefs = jnp.dot(hi, wa_hi[...], preferred_element_type=F32)
        coefs += jnp.dot(hi, wa_lo[...], preferred_element_type=F32)
        coefs += jnp.dot(lo, wa_hi[...], preferred_element_type=F32)
        coefs = jnp.where(mine, coefs, 0.0)
        dense = coefs[0:OWN]
        for j in range(1, TILES):
            dense += coefs[j * OWN : (j + 1) * OWN]
        quad[me4, g] = dense
        return c, moved, coefs

    def finish_momentum(g, c, moved, coefs):
        out_m[0, :, c] = moved - spread(coefs)
        s = pltpu.make_async_copy(out_m.at[:, :, c], new_momentum.at[:, :, c], store_sem.at[0, g])
        s.start()
        stores.append(s)

    BATCHES = [(0, 3), (3, 6), (6, 7)]
    q, v = {}, {}

    def quad_sends(b):
        g0, g1 = BATCHES[b]
        q[b] = []
        for t, d in enumerate(quads):
            part = quad.at[me4, pl.ds(g0, g1 - g0)]
            c = pltpu.make_async_remote_copy(
                src_ref=part, dst_ref=part, send_sem=quad_send.at[b, t], recv_sem=quad_recv.at[b, t],
                device_id=d, device_id_type=MESH,
            )
            c.start()
            q[b].append(c)

    def ring_sends(b):
        g0, g1 = BATCHES[b]
        for c in q[b]:
            c.wait_recv()
        s = slice(g0, g1)
        ring[z, s] = (quad[0, s] + quad[1, s]) + (quad[2, s] + quad[3, s])
        v[b] = []
        part = ring.at[z, pl.ds(g0, g1 - g0)]
        for t, d in enumerate(rings):
            c = pltpu.make_async_remote_copy(
                src_ref=part, dst_ref=part, send_sem=ring_send.at[b, t], recv_sem=ring_recv.at[b, t],
                device_id=d, device_id_type=MESH,
            )
            c.start()
            v[b].append(c)

    def weights(b):
        g0, g1 = BATCHES[b]
        for c in v[b]:
            c.wait_recv()
        for g in range(g0, g1):
            total = ring[0, g]
            for k in range(1, NZ):
                total += ring[k, g]
            mean = total * (1.0 / 32)
            rows = jnp.concatenate([mean] * TILES, axis=0)
            c = cols_of(g)
            out_w[:, c] = weight[:, c] - STEP_SIZE * spread(jnp.where(mine, rows, 0.0))
            s = pltpu.make_async_copy(out_w.at[:, c], new_weight.at[:, c], store_sem.at[1, g])
            s.start()
            stores.append(s)

    products(0)
    pl.semaphore_wait(barrier, len(friends))
    first_sends(0)
    x_one(0)
    for g in range(1, GROUPS):
        products(g)
        first_sends(g)
        if g < 4:
            x_one(g)
    for g in range(GROUPS):
        step_b(g)
        step_c(g, True)
        if g in (2, 4):
            x_one(4 if g == 2 else 5)
    picks()
    loads[2].wait()
    loads[3].wait()
    events = (
        [(17.4 + g, "c", g) for g in range(GROUPS)]
        + [(22.2 + g, "d", g) for g in range(GROUPS)]
        + [(25.5 + g, "e", g) for g in range(GROUPS)]
        + [(32.5 + g, "f", g) for g in range(GROUPS)]
        + [(23.45, "x1", 6)]
        + [(23.5 + 0.9 * g, "x0", g) for g in range(GROUPS)]
    )
    late = []
    for _, kind, g in sorted(events):
        if kind == "c":
            step_c(g, False)
        elif kind == "d":
            step_d(g)
        elif kind == "e":
            step_e(g)
        elif kind == "x1":
            x_one(g)
        elif kind == "x0":
            x_zero(g)
        else:
            held = step_f(g)
            for b, (g0, g1) in enumerate(BATCHES):
                if g == g1 - 1:
                    quad_sends(b)
            finish_momentum(g, *held)
            if g == 4:
                ring_sends(0)
    ring_sends(1)
    weights(0)
    ring_sends(2)
    weights(1)
    for c in sent:
        c.wait_send()
    for cs in (*q.values(), *v.values()):
        for c in cs:
            c.wait_send()
    weights(2)
    for s in stores:
        s.wait()


MESSAGES = 18 * GROUPS


def on_device(acts, cotangent, weight, momentum, bands):
    any_space = pl.BlockSpec(memory_space=pl.ANY)
    unit = lambda *lead: pltpu.VMEM((*lead, OWN, COLS), F32)
    dma = lambda *shape: pltpu.SemaphoreType.DMA(shape)
    return pl.pallas_call(
        kernel,
        out_shape=(
            jax.ShapeDtypeStruct((OWN, COLS), F32),
            jax.ShapeDtypeStruct((1, OWN, COLS), F32),
        ),
        in_specs=[pl.BlockSpec(memory_space=pltpu.SMEM)] + [any_space] * 5,
        out_specs=(any_space, any_space),
        scratch_shapes=[
            pltpu.VMEM((TOK, ROWS), BF16),
            pltpu.VMEM((TOK, COLS), BF16),
            unit(), unit(1),
            pltpu.VMEM((2, 2 * BAND, BAND), BF16),
            unit(), unit(1),
            unit(16), unit(2), unit(2), unit(2), unit(5), unit(), unit(), unit(), unit(),
            pltpu.VMEM((OWN * 128, 128), BF16), pltpu.VMEM((OWN * 128, 128), BF16),
            pltpu.VMEM((128, OWN * 128), BF16), pltpu.VMEM((128, OWN * 128), BF16),
            pltpu.VMEM((4, GROUPS, OWN, 128), F32), pltpu.VMEM((NZ, GROUPS, OWN, 128), F32),
            dma(4), dma(GROUPS), dma(2, GROUPS), dma(MESSAGES), dma(MESSAGES),
            dma(3, 3), dma(3, 3), dma(3, 7), dma(3, 7),
        ],
        compiler_params=pltpu.CompilerParams(
            collective_id=0, has_side_effects=True, vmem_limit_bytes=48 * 2**20
        ),
    )(bands, acts, cotangent, weight, momentum, jnp.asarray(table()))


def solution(mesh):
    placed = (
        P(("rep", "fsdp"), None),
        P(("rep", "fsdp"), None),
        P("fsdp", None),
        P("rep", "fsdp", None),
        P("fsdp", None),
    )
    return jax.shard_map(
        on_device,
        mesh=mesh,
        in_specs=placed,
        out_specs=(P("fsdp", None), P("rep", "fsdp", None)),
        check_vma=False,
    )
```

time: 311 us -> 67.8 us (0.22)
  waiting for transfers between devices: 171 us -> 0 us
  blocking collectives: 111 us -> 0 us
  Pallas kernels: 0 us -> 58.8 us
  between operations: 14.8 us -> 0.65 us
  matrix products: 7.02 us -> 0 us
  local copies, waits for them, and re-layouts: 2.9 us -> 7.64 us
    unnamed x2 -> x0, waiting for transfers between devices: 171 us -> none
    psum x1 -> x0, blocking collectives: 111 us -> none  [on_device(): total = lax.psum(coefs, 'rep')]
    pallas_call x0 -> x1, Pallas kernels: none -> 58.8 us  [on_device(): pl.pallas_call(kernel, out_shape=(jax.ShapeDtypeStruct((OWN, COLS), F32),...]
    dot_general x5 -> x0, matrix products: 7.02 us -> none  [the longest x1 4.51 us: on_device(): lax.dot_general(acts, cotangent, contract, preferred_element_type=jnp.flo...]
    unnamed x9 -> x13, local copies, waits for them, and re-layouts: 2.03 us -> 7.64 us
  transfers between devices with their start and end apart: 1 -> 0, of which waited for: 1 -> 0; matrix products, arithmetic and copies ran while one was open for 1% -> 0% of each run, Pallas kernels for 0% -> 0%
where the time goes in v1:
time: 67.8 us; the launch traced here: 67.1 us
  Pallas kernels  58.8 us (87%)
  local copies, waits for them, and re-layouts  7.64 us (11%)
    pallas_call x1, Pallas kernels, on_device(): pl.pallas_call(kernel, out_shape=(jax.ShapeDtypeStruct((OWN, COLS), F32),...  58.8 us
    unnamed x13, local copies, waits for them, and re-layouts  7.64 us

profile of v1, /device:TPU:1, one launch (start us, length us, event | category | flops | bytes accessed | tf_op | source)
XLA Modules:
  0.0 67.1 jit_solution(16846354596636841664)
XLA Ops:
  0.6 0.8 %copy.8.acts_hbm = bf16[128,64]{1,0:T(8,128)(2,1)S(1)} copy(bf16[128,64]{0,1:T(8,128)(2,1)} %param.6) | data formatting | bytes 32768 | tf_op args[0]
  1.5 0.0 copy-start
  1.5 2.0 %copy-done = bf16[128,14336]{1,0:T(8,128)(2,1)S(1)} copy-done((bf16[128,14336]{1,0:T(8,128)(2,1)S(1)}, bf16[128,14336]{1,0:T(8,128)(2,1)}, u32[]{:S(2)}) %copy-start) | copy-done | bytes 3670040
  3.5 0.0 copy-start.1
  3.5 0.9 %copy-done.1 = f32[4,14336]{1,0:T(4,128)S(1)} copy-done((f32[4,14336]{1,0:T(4,128)S(1)}, f32[4,14336]{1,0:T(4,128)}, u32[]{:S(2)}) %copy-start.1) | copy-done | bytes 229400
  4.4 0.0 copy-start.2
  4.4 0.9 %copy-done.2 = f32[1,4,14336]{2,1,0:T(4,128)S(1)} copy-done((f32[1,4,14336]{2,1,0:T(4,128)S(1)}, f32[1,4,14336]{2,1,0:T(4,128)}, u32[]{:S(2)}) %copy-start.2) | copy-done | bytes 229400
  5.4 0.0 copy-start.3
  5.4 0.8 %copy-done.3 = bf16[2,128,64]{2,1,0:T(8,128)(2,1)S(1)} copy-done((bf16[2,128,64]{2,1,0:T(8,128)(2,1)S(1)}, bf16[2,128,64]{2,1,0:T(8,128)(2,1)}, u32[]{:S(2)}) %copy-start.3) | copy-done | bytes 32792
  6.2 0.0 copy-start.4
  6.2 0.7 %copy-done.4 = s32[4,4]{1,0:T(4,128)S(1)} copy-done((s32[4,4]{1,0:T(4,128)S(1)}, s32[4,4]{1,0:T(4,128)}, u32[]{:S(2)}) %copy-start.4) | copy-done | bytes 88
  6.9 58.8 %shard_map.77 = (f32[4,14336]{1,0:T(4,128)S(1)}, f32[1,4,14336]{2,1,0:T(4,128)S(1)}) custom-call(s32[4,4]{1,0:T(4,128)S(1)} %copy-done.4, bf16[128,64]{1,0:T(8,128)(2,1)S(1)} %copy.8.acts_hbm, bf16[128,14336]{1,0:T(8,128)(2,1)S(1)} %copy-done, f32[4,14336]{1,0:T(4,128)S(1)} %copy-done.1, f32[1,4,14336]{2,1,0:T(4,128)S(1)} %copy-done.2, ...), custom_call_target="tpu_custom_call" | custom-call | tf_op jit(solution)/shard_map/pallas_call | solution.py:371
  65.7 0.7 %copy.11 = f32[4,14336]{1,0:T(4,128)} copy(f32[4,14336]{1,0:T(4,128)S(1)} %get-tuple-element.4) | data formatting | bytes 458752
  66.4 0.7 %copy.12 = f32[1,4,14336]{2,1,0:T(4,128)} copy(f32[1,4,14336]{2,1,0:T(4,128)S(1)} %get-tuple-element.5) | data formatting | bytes 458752
Async XLA Ops:
  1.5 2.0 %copy-start = (bf16[128,14336]{1,0:T(8,128)(2,1)S(1)}, bf16[128,14336]{1,0:T(8,128)(2,1)}, u32[]{:S(2)}) copy-start(bf16[128,14336]{1,0:T(8,128)(2,1)} %cot_hbm.1) | copy-start | bytes 11010052
  3.5 0.9 %copy-start.1 = (f32[4,14336]{1,0:T(4,128)S(1)}, f32[4,14336]{1,0:T(4,128)}, u32[]{:S(2)}) copy-start(f32[4,14336]{1,0:T(4,128)} %weight_hbm.1) | copy-start | bytes 688132
  4.4 0.9 %copy-start.2 = (f32[1,4,14336]{2,1,0:T(4,128)S(1)}, f32[1,4,14336]{2,1,0:T(4,128)}, u32[]{:S(2)}) copy-start(f32[1,4,14336]{2,1,0:T(4,128)} %momentum_hbm.1) | copy-start | bytes 688132
  5.4 0.8 %copy-start.3 = (bf16[2,128,64]{2,1,0:T(8,128)(2,1)S(1)}, bf16[2,128,64]{2,1,0:T(8,128)(2,1)}, u32[]{:S(2)}) copy-start(bf16[2,128,64]{2,1,0:T(8,128)(2,1)} %constant.2.clone.table_hbm) | copy-start | bytes 98308
  6.2 0.7 %copy-start.4 = (s32[4,4]{1,0:T(4,128)S(1)}, s32[4,4]{1,0:T(4,128)}, u32[]{:S(2)}) copy-start(s32[4,4]{1,0:T(4,128)} %bands.1) | copy-start | bytes 196

commit v2 on v0

v2 whole, which is shorter than its diff:
```python
import jax
import jax.numpy as jnp
import numpy as np
from jax import lax
from jax.experimental import pallas as pl
from jax.experimental.pallas import tpu as pltpu
from jax.sharding import PartitionSpec as P

MESH = pl.DeviceIdType.MESH
F32, BF16 = jnp.float32, jnp.bfloat16

TOK, COLS, ROWS, BAND, KEEP = 128, 14336, 64, 64, 4
NZ, NY = 8, 8
OWN = 4
OWNERS = ROWS // OWN
GROUP = 2048
GROUPS = COLS // GROUP
HALF = GROUP // 2
CHUNK = 512
TILES = GROUP // 128
BATCHES = [(0, 3), (3, 6), (6, 7)]

STEP_SIZE = 2.0
DECAY = 0.999


def table():
    band, place = np.arange(BAND)[None, :], np.arange(2 * BAND)[:, None] % BAND
    scale = np.where(band == 0, np.sqrt(1.0 / BAND), np.sqrt(2.0 / BAND))
    full = (scale * np.cos(np.pi * (2 * place + 1) * band / (2 * BAND))).astype(np.float32)
    high = full.astype(jnp.bfloat16)
    low = (full - high.astype(np.float32)).astype(jnp.bfloat16)
    return np.stack([high, low])


def cols_of(g, half=None):
    if half is None:
        return pl.ds(g * GROUP, GROUP)
    return pl.ds(g * GROUP + half * HALF, HALF)


def split(x):
    high = x.astype(BF16)
    return high, (x - high.astype(F32)).astype(BF16)


def iota(shape, axis):
    return lax.broadcasted_iota(jnp.int32, shape, axis)


def by_row(x):
    row = lax.rem(iota(x.shape, 0), OWN)
    return jnp.concatenate([jnp.where(row == i, x, 0.0) for i in range(OWN)], axis=1)


def own_lanes(x):
    tile = lax.rem(iota(x.shape, 0) // OWN, TILES)
    return jnp.where(tile == iota(x.shape, 1) // (2 * KEEP), x, 0.0)


def stacked(x):
    return jnp.concatenate([x[:, j * 128 : (j + 1) * 128] for j in range(x.shape[1] // 128)], axis=0)


def unstacked(x):
    return jnp.concatenate([x[j * OWN : (j + 1) * OWN] for j in range(x.shape[0] // OWN)], axis=1)


def kernel(
    bands_hbm, acts_hbm, cot_hbm, weight_hbm, momentum_hbm, table_hbm,
    new_weight, new_momentum,
    bands, acts, cot, weight, momentum, tab,
    term, got4, got3p, got3m, gotx, got2p, got2m, got1p, got1m,
    wa_hi, wa_lo, wb_hi, wb_lo, quad, ring,
    load_sem, cot_sem, recv, send, rep_recv, rep_send,
):
    rep, fsdp = lax.axis_index("rep"), lax.axis_index("fsdp")
    z, me4 = rep // 4, lax.rem(rep, 4)
    xlo, core = me4 // 2, lax.rem(me4, 2)
    xhi, y = fsdp // NY, lax.rem(fsdp, NY)

    up = (rep, xhi * NY + lax.rem(y + 1, NY))
    down = (rep, xhi * NY + lax.rem(y + NY - 1, NY))
    across = (rep, (1 - xhi) * NY + y)
    quads = [
        (z * 4 + 2 * xlo + (1 - core), fsdp),
        (z * 4 + 2 * (1 - xlo) + core, fsdp),
        (z * 4 + 2 * (1 - xlo) + (1 - core), fsdp),
    ]
    rings = [(lax.rem(z + t, NZ) * 4 + me4, fsdp) for t in (4, 3, 5, 2, 6, 1, 7)]

    loads = [
        pltpu.make_async_copy(src, dst, load_sem.at[i])
        for i, (src, dst) in enumerate(
            [(acts_hbm, acts), (table_hbm, tab), (momentum_hbm, momentum), (weight_hbm, weight), (bands_hbm, bands)]
        )
    ]
    cots = [
        pltpu.make_async_copy(cot_hbm.at[:, cols_of(g)], cot.at[:, cols_of(g)], cot_sem.at[g])
        for g in range(GROUPS)
    ]
    loads[0].start()
    for c in cots:
        c.start()
    for c in loads[1:]:
        c.start()

    barrier = pltpu.get_barrier_semaphore()
    friends = [up, down, across, *quads, *rings]
    for d in friends:
        pl.semaphore_signal(barrier, inc=1, device_id=d, device_id_type=MESH)

    def message(src, dst, device, kind, g):
        pltpu.make_async_remote_copy(
            src_ref=src, dst_ref=dst, send_sem=send.at[0], recv_sem=recv.at[kind, g],
            device_id=device, device_id_type=MESH,
        ).start()

    def landed(ref, sem):
        pltpu.make_async_copy(ref, ref, sem).wait()

    K4, K3F, K3D, KX, KE, KF = range(6)

    def products(g):
        cots[g].wait()
        for s in range(GROUP // CHUNK):
            at = pl.ds(g * GROUP + s * CHUNK, CHUNK)
            out = jnp.dot(acts[...], cot[:, at], preferred_element_type=F32)
            for o in range(OWNERS):
                r = xhi if o < NY else 1 - xhi
                u = 2 * lax.rem(o % NY - y + NY, NY) + r
                term[u, :, at] = out[o * OWN : (o + 1) * OWN]

    def first_sends(g):
        e, o = cols_of(g, 0), cols_of(g, 1)
        message(term.at[pl.ds(8, 2), :, e], got4.at[:, :, e], up, K4, g)
        message(term.at[pl.ds(8, 2), :, o], got4.at[:, :, o], down, K4, g)
        message(term.at[pl.ds(6, 2), :, o], got3p.at[:, :, o], up, K3F, g)
        message(term.at[pl.ds(10, 2), :, e], got3m.at[:, :, e], down, K3F, g)

    def x_one(g):
        c = cols_of(g)
        message(term.at[3, :, c], gotx.at[1, :, c], across, KE, g)
        message(term.at[15, :, c], gotx.at[4, :, c], across, KE, g)

    def x_zero(g):
        c = cols_of(g)
        message(term.at[1, :, c], gotx.at[0, :, c], across, KF, g)

    def step_b(g):
        e, o = cols_of(g, 0), cols_of(g, 1)
        landed(got4.at[:, :, cols_of(g)], recv.at[K4, g])
        term[6:8, :, e] += got4[:, :, e]
        message(term.at[pl.ds(6, 2), :, e], got3p.at[:, :, e], up, K3D, g)
        term[10:12, :, o] += got4[:, :, o]
        message(term.at[pl.ds(10, 2), :, o], got3m.at[:, :, o], down, K3D, g)

    def step_c(g, kind):
        landed(got3p.at[:, :, cols_of(g)], recv.at[kind, g])
        c = cols_of(g, 1 if kind == K3F else 0)
        term[5, :, c] += got3p[1, :, c]
        message(term.at[5, :, c], gotx.at[2, :, c], across, KX, g)
        term[4, :, c] += got3p[0, :, c]
        c = cols_of(g, 0 if kind == K3F else 1)
        term[13, :, c] += got3m[1, :, c]
        message(term.at[13, :, c], gotx.at[3, :, c], across, KX, g)
        term[12, :, c] += got3m[0, :, c]

    def step_d(g):
        c = cols_of(g)
        landed(gotx.at[pl.ds(2, 2), :, c], recv.at[KX, g])
        term[4, :, c] += gotx[2, :, c]
        message(term.at[4, :, c], got2p.at[:, c], up, KE, g)
        term[12, :, c] += gotx[3, :, c]
        message(term.at[12, :, c], got2m.at[:, c], down, KE, g)

    def step_e(g):
        c = cols_of(g)
        landed(gotx.at[pl.ds(1, 4), :, c], recv.at[KE, g])
        term[2, :, c] += got2p[:, c] + gotx[1, :, c]
        message(term.at[2, :, c], got1p.at[:, c], up, KF, g)
        term[14, :, c] += got2m[:, c] + gotx[4, :, c]
        message(term.at[14, :, c], got1m.at[:, c], down, KF, g)

    def picks():
        for c in loads[1:]:
            c.wait()
        lane, band = iota((BAND, 128), 1), iota((BAND, 128), 0)
        same = iota((128, 128), 0) // BAND == lax.rem(iota((128, 128), 1) // KEEP, 2)
        for i in range(OWN):
            want = jnp.zeros((BAND, 128), jnp.int32)
            for k in range(KEEP):
                want = jnp.where(lax.rem(lane, KEEP) == k, bands[i, k], want)
            onehot = (want == band).astype(BF16)
            for t, wa, wb in ((0, wa_hi, wb_hi), (1, wa_lo, wb_lo)):
                w = jnp.dot(tab[t], onehot, preferred_element_type=F32)
                w = jnp.where(same, w, 0.0).astype(BF16)
                wa[i * 128 : (i + 1) * 128, :] = w
                wb[:, i * 128 : (i + 1) * 128] = w

    def spread(coefs):
        hi, lo = split(by_row(coefs))
        nt = (((1,), (1,)), ((), ()))
        out = lax.dot_general(hi, wb_hi[...], nt, preferred_element_type=F32)
        out += lax.dot_general(hi, wb_lo[...], nt, preferred_element_type=F32)
        out += lax.dot_general(lo, wb_hi[...], nt, preferred_element_type=F32)
        return unstacked(out)

    held = {}

    def step_f(g):
        c = cols_of(g)
        landed(gotx.at[pl.ds(0, 3), :, c], recv.at[KF, g])
        grad = (term[0, :, c] + gotx[0, :, c]) + (got1p[:, c] + got1m[:, c])
        moved = DECAY * momentum[0, :, c] + grad
        hi, lo = split(by_row(stacked(moved)))
        coefs = jnp.dot(hi, wa_hi[...], preferred_element_type=F32)
        coefs += jnp.dot(hi, wa_lo[...], preferred_element_type=F32)
        coefs += jnp.dot(lo, wa_hi[...], preferred_element_type=F32)
        coefs = own_lanes(coefs)
        dense = coefs[0:OWN]
        for j in range(1, TILES):
            dense += coefs[j * OWN : (j + 1) * OWN]
        quad[me4, g] = dense
        held[g] = moved, coefs

    def finish_momentum(g):
        moved, coefs = held.pop(g)
        new_momentum[0, :, cols_of(g)] = moved - spread(coefs)

    def rep_message(ref, device, kind, b):
        pltpu.make_async_remote_copy(
            src_ref=ref, dst_ref=ref, send_sem=rep_send.at[kind], recv_sem=rep_recv.at[kind, b],
            device_id=device, device_id_type=MESH,
        ).start()

    def quad_sends(b):
        g0, g1 = BATCHES[b]
        for d in quads:
            rep_message(quad.at[me4, pl.ds(g0, g1 - g0)], d, 0, b)

    def ring_sends(b):
        g0, g1 = BATCHES[b]
        landed(quad.at[pl.ds(0, 3), pl.ds(g0, g1 - g0)], rep_recv.at[0, b])
        s = slice(g0, g1)
        ring[z, s] = (quad[0, s] + quad[1, s]) + (quad[2, s] + quad[3, s])
        for d in rings:
            rep_message(ring.at[z, pl.ds(g0, g1 - g0)], d, 1, b)

    def weights(b):
        g0, g1 = BATCHES[b]
        landed(ring.at[pl.ds(0, NZ - 1), pl.ds(g0, g1 - g0)], rep_recv.at[1, b])
        rows = []
        for g in range(g0, g1):
            total = ring[0, g]
            for k in range(1, NZ):
                total += ring[k, g]
            rows += [total * (1.0 / 32)] * TILES
        update = spread(own_lanes(jnp.concatenate(rows, axis=0)))
        c = pl.ds(g0 * GROUP, (g1 - g0) * GROUP)
        new_weight[:, c] = weight[:, c] - STEP_SIZE * update

    loads[0].wait()
    products(0)
    pl.semaphore_wait(barrier, len(friends))
    first_sends(0)
    x_one(0)
    for g in range(1, GROUPS):
        products(g)
        first_sends(g)
        if g < 4:
            x_one(g)
    for g in range(GROUPS):
        step_b(g)
        step_c(g, K3F)
        if g in (2, 4):
            x_one(4 if g == 2 else 5)
    picks()
    events = (
        [(17.4 + g, step_c, g, K3D) for g in range(GROUPS)]
        + [(22.2 + g, step_d, g) for g in range(GROUPS)]
        + [(25.5 + g, step_e, g) for g in range(GROUPS)]
        + [(32.5 + g, step_f, g) for g in range(GROUPS)]
        + [(32.55 + g1 - 1, quad_sends, b) for b, (_, g1) in enumerate(BATCHES)]
        + [(32.6 + g, finish_momentum, g) for g in range(GROUPS)]
        + [(23.45, x_one, 6)]
        + [(23.5 + 0.9 * g, x_zero, g) for g in range(GROUPS)]
        + [(38.57, ring_sends, 0), (38.8, ring_sends, 1), (38.9, ring_sends, 2)]
        + [(39 + b, weights, b) for b in range(len(BATCHES))]
    )
    for _, f, *args in sorted(events, key=lambda e: e[0]):
        f(*args)
    landed(term.at[pl.ds(0, 15)], send.at[0])
    landed(quad.at[pl.ds(0, 3)], rep_send.at[0])
    landed(ring.at[pl.ds(0, 7)], rep_send.at[1])


def hand_out(weight, momentum, new_weight, new_momentum, sem):
    copies = [
        pltpu.make_async_copy(weight, new_weight, sem.at[0]),
        pltpu.make_async_copy(momentum, new_momentum, sem.at[1]),
    ]
    for c in copies:
        c.start()
    for c in copies:
        c.wait()


def on_device(acts, cotangent, weight, momentum, bands):
    hbm = pl.BlockSpec(memory_space=pltpu.HBM)
    vmem = pl.BlockSpec(memory_space=pltpu.VMEM)
    unit = lambda *lead: pltpu.VMEM((*lead, OWN, COLS), F32)
    dma = lambda *shape: pltpu.SemaphoreType.DMA(shape)
    results = pl.pallas_call(
        kernel,
        out_shape=(pltpu.VMEM((OWN, COLS), F32), pltpu.VMEM((1, OWN, COLS), F32)),
        in_specs=[hbm] * 6,
        out_specs=(vmem, vmem),
        scratch_shapes=[
            pltpu.SMEM((OWN, KEEP), jnp.int32),
            pltpu.VMEM((ROWS, TOK), BF16),
            pltpu.VMEM((TOK, COLS), BF16),
            unit(), unit(1),
            pltpu.VMEM((2, 2 * BAND, BAND), BF16),
            unit(16), unit(2), unit(2), unit(2), unit(5), unit(), unit(), unit(), unit(),
            pltpu.VMEM((OWN * 128, 128), BF16), pltpu.VMEM((OWN * 128, 128), BF16),
            pltpu.VMEM((128, OWN * 128), BF16), pltpu.VMEM((128, OWN * 128), BF16),
            pltpu.VMEM((4, GROUPS, OWN, 128), F32), pltpu.VMEM((NZ, GROUPS, OWN, 128), F32),
            dma(5), dma(GROUPS), dma(6, GROUPS), dma(1), dma(2, len(BATCHES)), dma(2),
        ],
        compiler_params=pltpu.CompilerParams(
            collective_id=0, has_side_effects=True, vmem_limit_bytes=40 * 2**20
        ),
    )(*(pltpu.with_memory_space_constraint(a, pltpu.HBM) for a in (bands, acts.T, cotangent, weight, momentum, jnp.asarray(table()))))
    return pl.pallas_call(
        hand_out,
        out_shape=(
            jax.ShapeDtypeStruct((OWN, COLS), F32),
            jax.ShapeDtypeStruct((1, OWN, COLS), F32),
        ),
        in_specs=[pl.BlockSpec(memory_space=pl.ANY)] * 2,
        out_specs=(hbm, hbm),
        scratch_shapes=[dma(2)],
        compiler_params=pltpu.CompilerParams(vmem_limit_bytes=2**20),
    )(*(pltpu.with_memory_space_constraint(a, pltpu.VMEM) for a in results))


def solution(mesh):
    placed = (
        P(("rep", "fsdp"), None),
        P(("rep", "fsdp"), None),
        P("fsdp", None),
        P("rep", "fsdp", None),
        P("fsdp", None),
    )
    return jax.shard_map(
        on_device,
        mesh=mesh,
        in_specs=placed,
        out_specs=(P("fsdp", None), P("rep", "fsdp", None)),
        check_vma=False,
    )
```

time: 311 us -> 54.2 us (0.17)
  waiting for transfers between devices: 171 us -> 0 us
  blocking collectives: 111 us -> 0 us
  Pallas kernels: 0 us -> 53.4 us
  between operations: 14.8 us -> 0.64 us
  matrix products: 7.02 us -> 0 us
    unnamed x2 -> x0, waiting for transfers between devices: 171 us -> none
    psum x1 -> x0, blocking collectives: 111 us -> none  [on_device(): total = lax.psum(coefs, 'rep')]
    pallas_call x0 -> x2, Pallas kernels: none -> 53.4 us  [the longest x1 52.7 us: on_device(): pl.pallas_call(kernel, out_shape=(pltpu.VMEM((OWN, COLS), F32), pltpu.VME...]
    dot_general x5 -> x0, matrix products: 7.02 us -> none  [the longest x1 4.51 us: on_device(): lax.dot_general(acts, cotangent, contract, preferred_element_type=jnp.flo...]
  transfers between devices with their start and end apart: 1 -> 0, of which waited for: 1 -> 0; matrix products, arithmetic and copies ran while one was open for 1% -> 0% of each run, Pallas kernels for 0% -> 0%
where the time goes in v2:
time: 54.2 us; the launch traced here: 54.1 us
  Pallas kernels  53.4 us (99%)
  between operations  0.64 us (1%)
    pallas_call x1, Pallas kernels, on_device(): pl.pallas_call(kernel, out_shape=(pltpu.VMEM((OWN, COLS), F32), pltpu.VME...  52.7 us

profile of v2, /device:TPU:1, one launch (start us, length us, event | category | flops | bytes accessed | tf_op | source)
XLA Modules:
  0.0 54.1 jit_solution(7410982916695214983)
XLA Ops:
  0.6 52.7 %shard_map.77 = (f32[4,14336]{1,0:T(4,128)S(1)}, f32[1,4,14336]{2,1,0:T(4,128)S(1)}) custom-call(s32[4,4]{1,0:T(4,128)} %bands_hbm.1, bf16[64,128]{1,0:T(8,128)(2,1)} %bitcast.1, bf16[128,14336]{1,0:T(8,128)(2,1)} %cot_hbm.1, f32[4,14336]{1,0:T(4,128)} %weight_hbm.1, f32[1,4,14336]{2,1,0:T(4,128)} %momentum_hbm.1, bf16[2,128,64]{2,1,0:T(8,128)(2,1)} %constant.2.clone.table_hbm), custom_call_target="tpu_custom_call" | custom-call | tf_op jit(solution)/shard_map/pallas_call | solution.py:314
  53.3 0.8 %shard_map.78 = (f32[4,14336]{1,0:T(4,128)}, f32[1,4,14336]{2,1,0:T(4,128)}) custom-call(f32[4,14336]{1,0:T(4,128)S(1)} %get-tuple-element.4.weight, f32[1,4,14336]{2,1,0:T(4,128)S(1)} %get-tuple-element.5.momentum), custom_call_target="tpu_custom_call" | custom-call | tf_op jit(solution)/shard_map/pallas_call | solution.py:335

commit v3 on v2

--- a/solution.py
+++ b/solution.py
@@ -10,7 +10,9 @@
 F32, BF16 = jnp.float32, jnp.bfloat16
 
 TOK, COLS, ROWS, BAND, KEEP = 128, 14336, 64, 64, 4
-NZ, NY = 8, 8
+NY = 8
+CHIPS = 16
+FARTHEST_FIRST = (8, 9, 7, 6, 10, 5, 11, 4, 12, 3, 13, 2, 14, 1, 15)
 OWN = 4
 OWNERS = ROWS // OWN
 GROUP = 2048
@@ -71,23 +73,18 @@
     new_weight, new_momentum,
     bands, acts, cot, weight, momentum, tab,
     term, got4, got3p, got3m, gotx, got2p, got2m, got1p, got1m,
-    wa_hi, wa_lo, wb_hi, wb_lo, quad, ring,
-    load_sem, cot_sem, recv, send, rep_recv, rep_send,
+    wa_hi, wa_lo, wb_hi, wb_lo, pair, ring,
+    load_sem, cot_sem, recv, send, rep_recv, rep_send, there,
 ):
     rep, fsdp = lax.axis_index("rep"), lax.axis_index("fsdp")
-    z, me4 = rep // 4, lax.rem(rep, 4)
-    xlo, core = me4 // 2, lax.rem(me4, 2)
+    chip, core = rep // 2, lax.rem(rep, 2)
     xhi, y = fsdp // NY, lax.rem(fsdp, NY)
 
     up = (rep, xhi * NY + lax.rem(y + 1, NY))
     down = (rep, xhi * NY + lax.rem(y + NY - 1, NY))
     across = (rep, (1 - xhi) * NY + y)
-    quads = [
-        (z * 4 + 2 * xlo + (1 - core), fsdp),
-        (z * 4 + 2 * (1 - xlo) + core, fsdp),
-        (z * 4 + 2 * (1 - xlo) + (1 - core), fsdp),
-    ]
-    rings = [(lax.rem(z + t, NZ) * 4 + me4, fsdp) for t in (4, 3, 5, 2, 6, 1, 7)]
+    beside = (2 * chip + (1 - core), fsdp)
+    others = [(2 * lax.rem(chip + t, CHIPS) + core, fsdp) for t in FARTHEST_FIRST]
 
     loads = [
         pltpu.make_async_copy(src, dst, load_sem.at[i])
@@ -106,9 +103,38 @@
         c.start()
 
     barrier = pltpu.get_barrier_semaphore()
-    friends = [up, down, across, *quads, *rings]
-    for d in friends:
+    for d in (up, down, across):
         pl.semaphore_signal(barrier, inc=1, device_id=d, device_id_type=MESH)
+
+    def tell(sem, first, last):
+        @pl.loop(first, last)
+        def _(i):
+            pl.semaphore_signal(sem, inc=1, device_id=(2 * i + core, fsdp), device_id_type=MESH)
+
+    tell(barrier, chip + 1, CHIPS)
+
+    @pl.when(core == 0)
+    def _():
+        pl.semaphore_signal(barrier, inc=1, device_id=beside, device_id_type=MESH)
+
+    def enter():
+        pl.semaphore_wait(barrier, 3 + chip + core)
+
+    def answer():
+        tell(there.at[0], 0, chip)
+
+        @pl.when(core == 1)
+        def _():
+            pl.semaphore_signal(there.at[1], inc=1, device_id=beside, device_id_type=MESH)
+
+    def all_there():
+        @pl.when(core == 0)
+        def _():
+            pl.semaphore_wait(there.at[1], 1)
+
+        @pl.when(chip < CHIPS - 1)
+        def _():
+            pl.semaphore_wait(there.at[0], CHIPS - 1 - chip)
 
     def message(src, dst, device, kind, g):
         pltpu.make_async_remote_copy(
@@ -119,7 +145,7 @@
     def landed(ref, sem):
         pltpu.make_async_copy(ref, ref, sem).wait()
 
-    K4, K3F, K3D, KX, KE, KF = range(6)
+    K4, K3F, K3D, KXF, KXD, KE, KF = range(7)
 
     def products(g):
         cots[g].wait()
@@ -157,20 +183,22 @@
 
     def step_c(g, kind):
         landed(got3p.at[:, :, cols_of(g)], recv.at[kind, g])
+        then = KXF if kind == K3F else KXD
         c = cols_of(g, 1 if kind == K3F else 0)
         term[5, :, c] += got3p[1, :, c]
-        message(term.at[5, :, c], gotx.at[2, :, c], across, KX, g)
+        message(term.at[5, :, c], gotx.at[2, :, c], across, then, g)
         term[4, :, c] += got3p[0, :, c]
         c = cols_of(g, 0 if kind == K3F else 1)
         term[13, :, c] += got3m[1, :, c]
-        message(term.at[13, :, c], gotx.at[3, :, c], across, KX, g)
+        message(term.at[13, :, c], gotx.at[3, :, c], across, then, g)
         term[12, :, c] += got3m[0, :, c]
 
-    def step_d(g):
-        c = cols_of(g)
-        landed(gotx.at[pl.ds(2, 2), :, c], recv.at[KX, g])
+    def step_d(g, kind):
+        landed(gotx.at[pl.ds(2, 2), :, cols_of(g, 0)], recv.at[kind, g])
+        c = cols_of(g, 1 if kind == KXF else 0)
         term[4, :, c] += gotx[2, :, c]
         message(term.at[4, :, c], got2p.at[:, c], up, KE, g)
+        c = cols_of(g, 0 if kind == KXF else 1)
         term[12, :, c] += gotx[3, :, c]
         message(term.at[12, :, c], got2m.at[:, c], down, KE, g)
 
@@ -221,7 +249,7 @@
         dense = coefs[0:OWN]
         for j in range(1, TILES):
             dense += coefs[j * OWN : (j + 1) * OWN]
-        quad[me4, g] = dense
+        pair[core, g] = dense
         held[g] = moved, coefs
 
     def finish_momentum(g):
@@ -234,26 +262,25 @@
             device_id=device, device_id_type=MESH,
         ).start()
 
-    def quad_sends(b):
+    def pair_sends(b):
         g0, g1 = BATCHES[b]
-        for d in quads:
-            rep_message(quad.at[me4, pl.ds(g0, g1 - g0)], d, 0, b)
+        rep_message(pair.at[core, pl.ds(g0, g1 - g0)], beside, 0, b)
 
     def ring_sends(b):
         g0, g1 = BATCHES[b]
-        landed(quad.at[pl.ds(0, 3), pl.ds(g0, g1 - g0)], rep_recv.at[0, b])
+        landed(pair.at[0, pl.ds(g0, g1 - g0)], rep_recv.at[0, b])
         s = slice(g0, g1)
-        ring[z, s] = (quad[0, s] + quad[1, s]) + (quad[2, s] + quad[3, s])
-        for d in rings:
-            rep_message(ring.at[z, pl.ds(g0, g1 - g0)], d, 1, b)
+        ring[chip, s] = pair[0, s] + pair[1, s]
+        for d in others:
+            rep_message(ring.at[chip, pl.ds(g0, g1 - g0)], d, 1, b)
 
     def weights(b):
         g0, g1 = BATCHES[b]
-        landed(ring.at[pl.ds(0, NZ - 1), pl.ds(g0, g1 - g0)], rep_recv.at[1, b])
+        landed(ring.at[pl.ds(0, CHIPS - 1), pl.ds(g0, g1 - g0)], rep_recv.at[1, b])
         rows = []
         for g in range(g0, g1):
             total = ring[0, g]
-            for k in range(1, NZ):
+            for k in range(1, CHIPS):
                 total += ring[k, g]
             rows += [total * (1.0 / 32)] * TILES
         update = spread(own_lanes(jnp.concatenate(rows, axis=0)))
@@ -262,37 +289,37 @@
 
     loads[0].wait()
     products(0)
-    pl.semaphore_wait(barrier, len(friends))
+    enter()
     first_sends(0)
     x_one(0)
+    answer()
     for g in range(1, GROUPS):
         products(g)
         first_sends(g)
         if g < 4:
             x_one(g)
-    for g in range(GROUPS):
-        step_b(g)
-        step_c(g, K3F)
-        if g in (2, 4):
-            x_one(4 if g == 2 else 5)
-    picks()
     events = (
-        [(17.4 + g, step_c, g, K3D) for g in range(GROUPS)]
-        + [(22.2 + g, step_d, g) for g in range(GROUPS)]
-        + [(25.5 + g, step_e, g) for g in range(GROUPS)]
-        + [(32.5 + g, step_f, g) for g in range(GROUPS)]
-        + [(32.55 + g1 - 1, quad_sends, b) for b, (_, g1) in enumerate(BATCHES)]
-        + [(32.6 + g, finish_momentum, g) for g in range(GROUPS)]
-        + [(23.45, x_one, 6)]
-        + [(23.5 + 0.9 * g, x_zero, g) for g in range(GROUPS)]
-        + [(38.57, ring_sends, 0), (38.8, ring_sends, 1), (38.9, ring_sends, 2)]
-        + [(39 + b, weights, b) for b in range(len(BATCHES))]
+        [(3.7 + 2 * g, step_b, g) for g in range(GROUPS)]
+        + [(4.7 + 2 * g, step_c, g, K3F) for g in range(GROUPS)]
+        + [(12.8, x_one, 4), (16.9, picks)]
+        + [(17.0 + 1.3 * g, step_d, g, KXF) for g in range(GROUPS)]
+        + [(19.0 + 1.3 * g, step_c, g, K3D) for g in range(GROUPS)]
+        + [(27.05, x_one, 5), (27.1, x_one, 6)]
+        + [(28 + g, step_d, g, KXD) for g in range(GROUPS)]
+        + [(28.1 + g, x_zero, g) for g in range(GROUPS)]
+        + [(35 + g, step_e, g) for g in range(GROUPS)]
+        + [(42.4, all_there)]
+        + [(42.5 + g, step_f, g) for g in range(GROUPS)]
+        + [(42.55 + g1 - 1, pair_sends, b) for b, (_, g1) in enumerate(BATCHES)]
+        + [(42.6 + g, finish_momentum, g) for g in range(GROUPS)]
+        + [(45.58, ring_sends, 0), (48.56, ring_sends, 1), (48.9, ring_sends, 2)]
+        + [(49 + b, weights, b) for b in range(len(BATCHES))]
     )
     for _, f, *args in sorted(events, key=lambda e: e[0]):
         f(*args)
     landed(term.at[pl.ds(0, 15)], send.at[0])
-    landed(quad.at[pl.ds(0, 3)], rep_send.at[0])
-    landed(ring.at[pl.ds(0, 7)], rep_send.at[1])
+    landed(pair.at[0], rep_send.at[0])
+    landed(ring.at[pl.ds(0, CHIPS - 1)], rep_send.at[1])
 
 
 def hand_out(weight, momentum, new_weight, new_momentum, sem):
@@ -325,8 +352,8 @@
             unit(16), unit(2), unit(2), unit(2), unit(5), unit(), unit(), unit(), unit(),
             pltpu.VMEM((OWN * 128, 128), BF16), pltpu.VMEM((OWN * 128, 128), BF16),
             pltpu.VMEM((128, OWN * 128), BF16), pltpu.VMEM((128, OWN * 128), BF16),
-            pltpu.VMEM((4, GROUPS, OWN, 128), F32), pltpu.VMEM((NZ, GROUPS, OWN, 128), F32),
-            dma(5), dma(GROUPS), dma(6, GROUPS), dma(1), dma(2, len(BATCHES)), dma(2),
+            pltpu.VMEM((2, GROUPS, OWN, 128), F32), pltpu.VMEM((CHIPS, GROUPS, OWN, 128), F32),
+            dma(5), dma(GROUPS), dma(7, GROUPS), dma(1), dma(2, len(BATCHES)), dma(2), pltpu.SemaphoreType.REGULAR((2,)),
         ],
         compiler_params=pltpu.CompilerParams(
             collective_id=0, has_side_effects=True, vmem_limit_bytes=40 * 2**20

time: 54.2 us -> 51.8 us (0.956)
  Pallas kernels: 53.4 us -> 51 us
    pallas_call x1, Pallas kernels: 52.7 us -> 50.3 us  [on_device(): pl.pallas_call(kernel, out_shape=(pltpu.VMEM((OWN, COLS), F32), pltpu.VME...]
where the time goes in v3:
time: 51.8 us; the launch traced here: 51.7 us
  Pallas kernels  51 us (98%)
  between operations  0.64 us (1%)
    pallas_call x1, Pallas kernels, on_device(): pl.pallas_call(kernel, out_shape=(pltpu.VMEM((OWN, COLS), F32), pltpu.VME...  50.3 us

profile of v3, /device:TPU:1, one launch (start us, length us, event | category | flops | bytes accessed | tf_op | source)
XLA Modules:
  0.0 51.7 jit_solution(12371409490144277018)
XLA Ops:
  0.6 50.3 %shard_map.77 = (f32[4,14336]{1,0:T(4,128)S(1)}, f32[1,4,14336]{2,1,0:T(4,128)S(1)}) custom-call(s32[4,4]{1,0:T(4,128)} %bands_hbm.1, bf16[64,128]{1,0:T(8,128)(2,1)} %bitcast.1, bf16[128,14336]{1,0:T(8,128)(2,1)} %cot_hbm.1, f32[4,14336]{1,0:T(4,128)} %weight_hbm.1, f32[1,4,14336]{2,1,0:T(4,128)} %momentum_hbm.1, bf16[2,128,64]{2,1,0:T(8,128)(2,1)} %constant.2.clone.table_hbm), custom_call_target="tpu_custom_call" | custom-call | tf_op jit(solution)/shard_map/pallas_call | solution.py:341
  50.9 0.8 %shard_map.78 = (f32[4,14336]{1,0:T(4,128)}, f32[1,4,14336]{2,1,0:T(4,128)}) custom-call(f32[4,14336]{1,0:T(4,128)S(1)} %get-tuple-element.4.weight, f32[1,4,14336]{2,1,0:T(4,128)S(1)} %get-tuple-element.5.momentum), custom_call_target="tpu_custom_call" | custom-call | tf_op jit(solution)/shard_map/pallas_call | solution.py:362

commit v4 on v3

--- a/solution.py
+++ b/solution.py
@@ -20,7 +20,7 @@
 HALF = GROUP // 2
 CHUNK = 512
 TILES = GROUP // 128
-BATCHES = [(0, 3), (3, 6), (6, 7)]
+BATCHES = [(0, 2), (2, 4), (4, 6), (6, 7)]
 
 STEP_SIZE = 2.0
 DECAY = 0.999
@@ -73,7 +73,7 @@
     new_weight, new_momentum,
     bands, acts, cot, weight, momentum, tab,
     term, got4, got3p, got3m, gotx, got2p, got2m, got1p, got1m,
-    wa_hi, wa_lo, wb_hi, wb_lo, pair, ring,
+    wa, wb, kept, pair, ring,
     load_sem, cot_sem, recv, send, rep_recv, rep_send, there,
 ):
     rep, fsdp = lax.axis_index("rep"), lax.axis_index("fsdp")
@@ -93,11 +93,11 @@
         )
     ]
     cots = [
-        pltpu.make_async_copy(cot_hbm.at[:, cols_of(g)], cot.at[:, cols_of(g)], cot_sem.at[g])
-        for g in range(GROUPS)
+        pltpu.make_async_copy(cot_hbm.at[:, c], cot.at[:, c], cot_sem.at[i])
+        for i, c in enumerate([cols_of(0, 0), *map(cols_of, range(1, GROUPS)), cols_of(0, 1)])
     ]
     loads[0].start()
-    for c in cots:
+    for c in (cots[0], cots[GROUPS], *cots[1:GROUPS]):
         c.start()
     for c in loads[1:]:
         c.start()
@@ -147,22 +147,25 @@
 
     K4, K3F, K3D, KXF, KXD, KE, KF = range(7)
 
-    def products(g):
-        cots[g].wait()
-        for s in range(GROUP // CHUNK):
-            at = pl.ds(g * GROUP + s * CHUNK, CHUNK)
+    def products(g, half):
+        if half == 0 or g == 0:
+            cots[g if half == 0 else GROUPS].wait()
+        for s in range(HALF // CHUNK):
+            at = pl.ds(g * GROUP + half * HALF + s * CHUNK, CHUNK)
             out = jnp.dot(acts[...], cot[:, at], preferred_element_type=F32)
             for o in range(OWNERS):
                 r = xhi if o < NY else 1 - xhi
                 u = 2 * lax.rem(o % NY - y + NY, NY) + r
                 term[u, :, at] = out[o * OWN : (o + 1) * OWN]
 
-    def first_sends(g):
-        e, o = cols_of(g, 0), cols_of(g, 1)
-        message(term.at[pl.ds(8, 2), :, e], got4.at[:, :, e], up, K4, g)
-        message(term.at[pl.ds(8, 2), :, o], got4.at[:, :, o], down, K4, g)
-        message(term.at[pl.ds(6, 2), :, o], got3p.at[:, :, o], up, K3F, g)
-        message(term.at[pl.ds(10, 2), :, e], got3m.at[:, :, e], down, K3F, g)
+    def first_sends(g, half):
+        c = cols_of(g, half)
+        if half == 0:
+            message(term.at[pl.ds(8, 2), :, c], got4.at[:, :, c], up, K4, g)
+            message(term.at[pl.ds(10, 2), :, c], got3m.at[:, :, c], down, K3F, g)
+        else:
+            message(term.at[pl.ds(8, 2), :, c], got4.at[:, :, c], down, K4, g)
+            message(term.at[pl.ds(6, 2), :, c], got3p.at[:, :, c], up, K3F, g)
 
     def x_one(g):
         c = cols_of(g)
@@ -220,21 +223,21 @@
             for k in range(KEEP):
                 want = jnp.where(lax.rem(lane, KEEP) == k, bands[i, k], want)
             onehot = (want == band).astype(BF16)
-            for t, wa, wb in ((0, wa_hi, wb_hi), (1, wa_lo, wb_lo)):
+            for t, places in ((0, (0, 2)), (1, (1,))):
                 w = jnp.dot(tab[t], onehot, preferred_element_type=F32)
                 w = jnp.where(same, w, 0.0).astype(BF16)
-                wa[i * 128 : (i + 1) * 128, :] = w
-                wb[:, i * 128 : (i + 1) * 128] = w
+                for p in places:
+                    at = slice((p * OWN + i) * 128, (p * OWN + i + 1) * 128)
+                    wa[at, :] = w
+                    wb[:, at] = w
 
     def spread(coefs):
         hi, lo = split(by_row(coefs))
         nt = (((1,), (1,)), ((), ()))
-        out = lax.dot_general(hi, wb_hi[...], nt, preferred_element_type=F32)
-        out += lax.dot_general(hi, wb_lo[...], nt, preferred_element_type=F32)
-        out += lax.dot_general(lo, wb_hi[...], nt, preferred_element_type=F32)
+        out = lax.dot_general(
+            jnp.concatenate([hi, hi, lo], axis=1), wb[...], nt, preferred_element_type=F32
+        )
         return unstacked(out)
-
-    held = {}
 
     def step_f(g):
         c = cols_of(g)
@@ -242,19 +245,20 @@
         grad = (term[0, :, c] + gotx[0, :, c]) + (got1p[:, c] + got1m[:, c])
         moved = DECAY * momentum[0, :, c] + grad
         hi, lo = split(by_row(stacked(moved)))
-        coefs = jnp.dot(hi, wa_hi[...], preferred_element_type=F32)
-        coefs += jnp.dot(hi, wa_lo[...], preferred_element_type=F32)
-        coefs += jnp.dot(lo, wa_hi[...], preferred_element_type=F32)
-        coefs = own_lanes(coefs)
+        coefs = own_lanes(
+            jnp.dot(jnp.concatenate([hi, hi, lo], axis=1), wa[...], preferred_element_type=F32)
+        )
         dense = coefs[0:OWN]
         for j in range(1, TILES):
             dense += coefs[j * OWN : (j + 1) * OWN]
         pair[core, g] = dense
-        held[g] = moved, coefs
-
-    def finish_momentum(g):
-        moved, coefs = held.pop(g)
-        new_momentum[0, :, cols_of(g)] = moved - spread(coefs)
+        kept[g] = coefs
+        new_momentum[0, :, c] = moved
+
+    def finish_momentum(g0, g1):
+        c = pl.ds(g0 * GROUP, (g1 - g0) * GROUP)
+        coefs = kept[g0:g1].reshape((g1 - g0) * OWN * TILES, 128)
+        new_momentum[0, :, c] -= spread(coefs)
 
     def rep_message(ref, device, kind, b):
         pltpu.make_async_remote_copy(
@@ -288,14 +292,17 @@
         new_weight[:, c] = weight[:, c] - STEP_SIZE * update
 
     loads[0].wait()
-    products(0)
+    products(0, 0)
     enter()
-    first_sends(0)
+    first_sends(0, 0)
+    products(0, 1)
+    first_sends(0, 1)
     x_one(0)
     answer()
     for g in range(1, GROUPS):
-        products(g)
-        first_sends(g)
+        for half in range(2):
+            products(g, half)
+            first_sends(g, half)
         if g < 4:
             x_one(g)
     events = (
@@ -311,8 +318,8 @@
         + [(42.4, all_there)]
         + [(42.5 + g, step_f, g) for g in range(GROUPS)]
         + [(42.55 + g1 - 1, pair_sends, b) for b, (_, g1) in enumerate(BATCHES)]
-        + [(42.6 + g, finish_momentum, g) for g in range(GROUPS)]
-        + [(45.58, ring_sends, 0), (48.56, ring_sends, 1), (48.9, ring_sends, 2)]
+        + [(48.91, finish_momentum, 0, 4), (48.92, finish_momentum, 4, GROUPS)]
+        + [(44.58, ring_sends, 0), (46.58, ring_sends, 1), (48.56, ring_sends, 2), (48.9, ring_sends, 3)]
         + [(49 + b, weights, b) for b in range(len(BATCHES))]
     )
     for _, f, *args in sorted(events, key=lambda e: e[0]):
@@ -350,10 +357,10 @@
             unit(), unit(1),
             pltpu.VMEM((2, 2 * BAND, BAND), BF16),
             unit(16), unit(2), unit(2), unit(2), unit(5), unit(), unit(), unit(), unit(),
-            pltpu.VMEM((OWN * 128, 128), BF16), pltpu.VMEM((OWN * 128, 128), BF16),
-            pltpu.VMEM((128, OWN * 128), BF16), pltpu.VMEM((128, OWN * 128), BF16),
+            pltpu.VMEM((3 * OWN * 128, 128), BF16), pltpu.VMEM((128, 3 * OWN * 128), BF16),
+            pltpu.VMEM((GROUPS, OWN * TILES, 128), F32),
             pltpu.VMEM((2, GROUPS, OWN, 128), F32), pltpu.VMEM((CHIPS, GROUPS, OWN, 128), F32),
-            dma(5), dma(GROUPS), dma(7, GROUPS), dma(1), dma(2, len(BATCHES)), dma(2), pltpu.SemaphoreType.REGULAR((2,)),
+            dma(5), dma(GROUPS + 1), dma(7, GROUPS), dma(1), dma(2, len(BATCHES)), dma(2), pltpu.SemaphoreType.REGULAR((2,)),
         ],
         compiler_params=pltpu.CompilerParams(
             collective_id=0, has_side_effects=True, vmem_limit_bytes=40 * 2**20

time: 51.8 us -> 51.2 us (0.988)
  Pallas kernels: 51 us -> 50.4 us
    pallas_call x1, Pallas kernels: 50.3 us -> 49.6 us  [on_device(): pl.pallas_call(kernel, out_shape=(pltpu.VMEM((OWN, COLS), F32), pltpu.VME...]
where the time goes in v4:
time: 51.2 us; the launch traced here: 51 us
  Pallas kernels  50.4 us (98%)
  between operations  0.64 us (1%)
    pallas_call x1, Pallas kernels, on_device(): pl.pallas_call(kernel, out_shape=(pltpu.VMEM((OWN, COLS), F32), pltpu.VME...  49.6 us

profile of v4, /device:TPU:1, one launch (start us, length us, event | category | flops | bytes accessed | tf_op | source)
XLA Modules:
  0.0 51.0 jit_solution(13059104987314345102)
XLA Ops:
  0.6 49.6 %shard_map.77 = (f32[4,14336]{1,0:T(4,128)S(1)}, f32[1,4,14336]{2,1,0:T(4,128)S(1)}) custom-call(s32[4,4]{1,0:T(4,128)} %bands_hbm.1, bf16[64,128]{1,0:T(8,128)(2,1)} %bitcast.1, bf16[128,14336]{1,0:T(8,128)(2,1)} %cot_hbm.1, f32[4,14336]{1,0:T(4,128)} %weight_hbm.1, f32[1,4,14336]{2,1,0:T(4,128)} %momentum_hbm.1, bf16[2,128,64]{2,1,0:T(8,128)(2,1)} %constant.2.clone.table_hbm), custom_call_target="tpu_custom_call" | custom-call | tf_op jit(solution)/shard_map/pallas_call | solution.py:348
  50.3 0.8 %shard_map.78 = (f32[4,14336]{1,0:T(4,128)}, f32[1,4,14336]{2,1,0:T(4,128)}) custom-call(f32[4,14336]{1,0:T(4,128)S(1)} %get-tuple-element.4.weight, f32[1,4,14336]{2,1,0:T(4,128)S(1)} %get-tuple-element.5.momentum), custom_call_target="tpu_custom_call" | custom-call | tf_op jit(solution)/shard_map/pallas_call | solution.py:369
